TPU v7x, 32 devices: a whole 2x2x4 slice. The times are simulated.
32 devices in a mesh: expert: 8 (over z, y), grid: 4 (over x, core).
Axes of the slice: x: 2, y: 2, z: 4, core: 2. Of those that a mesh axis runs over, the one named last changes fastest.
Arguments:
- tokens: bfloat16 [4096, 1024], P(('expert', 'grid')), may hold values from -6 to 6
- routes: int32 [4096, 2], P(('expert', 'grid')), may hold values from 0 to 7, all different within a row; in each aligned block of 128 rows (0 to 127, 128 to 255, ...) at most 64 rows name the same one
- route_gates: float32 [4096, 2], P(('expert', 'grid')), may hold values from 0.2 to 1
- caption_lengths: int32 [32, 4], P(('expert', 'grid')), may hold values from 1 to 64, 128 in all within a row
- image_embed: bfloat16 [128, 1024], P(('expert', 'grid')), may hold values from -6 to 6
- final_gain: float32 [1024], replicated, may hold values from 0.1 to 1.9
- up_weight: bfloat16 [8, 1024, 4096], P('expert', None, 'grid'), may hold values from -0.1875 to 0.1875
- down_weight: bfloat16 [8, 1024, 4096], P('expert', None, 'grid'), may hold values from -0.09375 to 0.09375
Outputs:
- text_embed: float32 [128, 1024], P(('expert', 'grid'))
- sentence_direction_slope: float32 [128, 1024], P(('expert', 'grid'))
- picture_direction_slope: float32 [128, 1024], P(('expert', 'grid'))
Inputs may be any that keep to these rules, and one draw needn't show every extreme that they name: `routes`: each token names two different experts; among the 128 tokens of one device no expert is named more than 64 times, and in every draw some device names some expert exactly 64 times. `caption_lengths`: each row gives the token counts of one device's 4 captions, summing to 128; the largest of a row is exactly 64.
All inputs are finite; a program needn't handle non-finite values.
Results may differ from a plain program's by a relative error of at most 0.003.
Values may be sent and summed in bfloat16 or wider, within the bound.
A program may use at most 64 MiB of HBM per device.

v0:
```python
import functools
import math

import jax
import jax.numpy as jnp
from jax import lax
from jax.experimental import pallas as pl
from jax.experimental.pallas import tpu as pltpu
from jax.sharding import PartitionSpec as P

EPSILON = 1e-06
SIMILARITY_HEAT = 10.0
MESH = pl.DeviceIdType.MESH
BF16 = jnp.bfloat16
F32 = jnp.float32


def layer_norm(values):
    centred = values - jnp.mean(values, axis=-1, keepdims=True)
    return centred * lax.rsqrt(jnp.mean(centred * centred, axis=-1, keepdims=True) + EPSILON)


def root_norm(values):
    return values * lax.rsqrt(jnp.mean(values * values, axis=-1, keepdims=True) + EPSILON)


def flip(one, other, count):
    total, bit = 0, 1
    while bit < count:
        total = total + bit * (((one // bit) + (other // bit)) % 2)
        bit *= 2
    return total


def halves(values):
    high = values.astype(BF16)
    return high, (values - high.astype(F32)).astype(BF16)


def dot(left, right):
    return jnp.dot(left, right, preferred_element_type=F32)


def dot_nt(left, right):
    return lax.dot_general(left, right, (((1,), (1,)), ((), ())), preferred_element_type=F32)


def join(values, rows):
    width = values.shape[-1]
    if values.shape[-2] % 16 == 0:
        return values.reshape(rows, width)
    return values.astype(F32).reshape(rows, width).astype(values.dtype)


def part(values, lead):
    return values.reshape(lead + (values.shape[0] // math.prod(lead), values.shape[-1]))


def gelu(values):
    size = jnp.abs(values)
    t = 1.0 / (1.0 + (0.3275911 * math.sqrt(0.5)) * size)
    series = 0.5 * 1.061405429
    for term in (-1.453152027, 1.421413741, -0.284496736, 0.254829592):
        series = series * t + 0.5 * term
    tail = series * t * jnp.exp(values * values * -0.5)
    return jnp.maximum(values, 0.0) - size * tail


def slope(own, every, offset):
    logits = SIMILARITY_HEAT * dot_nt(own, every)
    row = lax.broadcasted_iota(jnp.int32, logits.shape, 0)
    column = lax.broadcasted_iota(jnp.int32, logits.shape, 1)
    signs = jnp.where(column == row + offset, 1.0, -1.0).astype(F32)
    coeff = -signs * jax.nn.sigmoid(-signs * logits)
    high, low = halves(coeff)
    return SIMILARITY_HEAT * (dot(high, every) + dot(low, every))


def kernel(
    experts, grids, slots, captions,
    lengths_ref, tokens_ref, routes_ref, gates_ref, image_ref, gain_ref, up_hbm, down_hbm,
    out_ref,
    up_ref, down_ref, down_turned, send, gate_high, gate_low, rows, own, part_send, part_in, sum_send, sum_in,
    back_send, back_in, own_image, near_image, all_image, own_text, near_text, all_text,
    weight_sem, to_expert_s, to_expert_r, fx_s, fx_r, fc_s, fc_r, part_s, part_r, sum_s, sum_r,
    back_s, back_r, near_s, near_r, far_s, far_r, across_r, spread_r,
):
    e = lax.axis_index("expert")
    g = lax.axis_index("grid")
    core = (e, g + 1 - 2 * (g % 2))
    cross = (e, (g + grids // 2) % grids)
    tokens, width = tokens_ref.shape
    group = grids * captions

    half = experts // 2

    def order(position):
        turned = position + experts - 1
        turn_of = turned % experts
        pair, odd = turn_of // 2 + 1, turn_of % 2
        return (turned // experts) * ((1 - odd) * pair + odd * (half + pair % half))

    opposite = ((e + half) % experts, g)

    def near_peer(step):
        return (flip(e, step, experts), g)

    def expert_peer(step):
        return (flip(e, order(step), experts), g)

    def push(source, target, send_sem, recv_sem, device):
        pltpu.make_async_remote_copy(
            src_ref=source, dst_ref=target, send_sem=send_sem, recv_sem=recv_sem,
            device_id=device, device_id_type=MESH,
        ).start()

    def await_bytes(ref, sem):
        pltpu.make_async_copy(ref, ref, sem).wait()

    barrier = pltpu.get_barrier_semaphore()

    def greet(step, carry):
        pl.semaphore_signal(barrier, inc=1, device_id=expert_peer(step), device_id_type=MESH)
        return carry

    lax.fori_loop(1, experts, greet, 0)
    for hop in range(1, grids):
        pl.semaphore_signal(barrier, inc=1, device_id=(e, (g + hop) % grids), device_id_type=MESH)
    load_up = pltpu.make_async_copy(up_hbm, up_ref, weight_sem.at[0])
    load_up.start()
    load_down = pltpu.make_async_copy(down_hbm, down_ref, weight_sem.at[1])
    load_down.start()

    normed = layer_norm(tokens_ref[...].astype(F32)).astype(BF16)
    routes = routes_ref[...]
    first, second = routes[0:1, :], routes[1:2, :]
    ids = lax.broadcasted_iota(jnp.int32, (max(experts, 8), tokens), 0)
    named = ((ids == first) | (ids == second)).astype(F32).astype(BF16)
    before = lax.broadcasted_iota(jnp.int32, (tokens, tokens), 0)
    after = lax.broadcasted_iota(jnp.int32, (tokens, tokens), 1)
    ranks = dot(named, (before < after).astype(F32).astype(BF16))
    spots = lax.broadcasted_iota(jnp.int32, (experts * slots, tokens), 0)
    hits = []
    for chosen in (first, second):
        rank = jnp.sum(jnp.where(ids == chosen, ranks, 0.0), axis=0, keepdims=True)
        far = flip(chosen, e, experts)
        spot_of = jnp.where(far > half, 2 * (far - half), jnp.maximum(2 * far - 1, 0))
        hits.append(spots == spot_of * slots + rank.astype(jnp.int32))
    taken = (hits[0] | hits[1]).astype(F32).astype(BF16)
    blocks = part(dot(taken, normed), (experts,)).astype(BF16)
    send[...] = blocks
    rows[0, 0] = blocks[0]
    pl.semaphore_wait(barrier, experts + grids - 2)

    def dispatch(step, carry):
        push(send.at[step], rows.at[step, 0], to_expert_s, to_expert_r.at[step], expert_peer(step))
        return carry

    ahead = min(4, experts)
    lax.fori_loop(1, ahead, dispatch, 0)
    push(rows.at[0, 0], rows.at[0, 1], fx_s, fx_r.at[0], cross)
    push(rows.at[0, 0], rows.at[0, 2], fc_s, fc_r.at[0], core)
    weights = jnp.where(hits[0], gates_ref[0:1, :], 0.0) + jnp.where(hits[1], gates_ref[1:2, :], 0.0)
    high, low = halves(weights.T)
    gate_high[...] = high
    gate_low[...] = low

    line = lax.broadcasted_iota(jnp.int32, (2 * group, 1), 0)
    caption = jnp.where(line < group, line - g * captions, line - group)
    images = root_norm(image_ref[...].astype(F32)) / math.sqrt(width)
    spread = jnp.zeros((2 * group, width), F32)
    for index in range(captions):
        spread = jnp.where(caption == index, images[index:index + 1, :], spread)
    near_image[0] = spread[:group].astype(BF16)
    own_image[...] = spread[group:].astype(BF16)

    def share_near(near, index):
        for hop in range(1, grids):
            push(near.at[0], near.at[hop], near_s.at[index], near_r.at[index], (e, (g + hop) % grids))

    def share_far(near, every, index):
        await_bytes(near.at[pl.ds(1, grids - 1)], near_r.at[index])
        total = near[0].astype(F32)
        for hop in range(1, grids):
            total = total + near[hop].astype(F32)
        every[0] = total.astype(BF16)

        push(every.at[0], every.at[half], far_s.at[index], across_r.at[index], opposite)

        def each(step, carry):
            push(every.at[0], every.at[step], far_s.at[index], far_r.at[index], near_peer(step))
            return carry

        lax.fori_loop(1, half, each, 0)

    def spread_far(every, index):
        await_bytes(every.at[half], across_r.at[index])

        def each(step, carry):
            push(
                every.at[half], every.at[half + step], far_s.at[index], spread_r.at[index],
                near_peer(step),
            )
            return carry

        lax.fori_loop(1, half, each, 0)

    def await_far(every, index):
        await_bytes(every.at[pl.ds(1, half - 1)], far_r.at[index])
        await_bytes(every.at[pl.ds(half + 1, half - 1)], spread_r.at[index])

    share_near(near_image, 0)

    tile = up_ref.shape[1] // 4

    def turn(index, carry):
        @pl.when(index + ahead < experts)
        def _():
            dispatch(index + ahead, 0)

        @pl.when((index > 0) & (index < experts))
        def _():
            at = index
            await_bytes(rows.at[at, 0], to_expert_r.at[at])
            push(rows.at[at, 0], rows.at[at, 1], fx_s, fx_r.at[at], cross)
            push(rows.at[at, 0], rows.at[at, 2], fc_s, fc_r.at[at], core)

        @pl.when((index >= 2) & (index < experts + 2))
        def _():
            at = index - 2
            await_bytes(rows.at[at, 1], fx_r.at[at])
            push(rows.at[at, 1], rows.at[at, 3], fc_s, fc_r.at[at], core)

        @pl.when(index == 1)
        def _():
            share_far(near_image, all_image, 0)
            load_up.wait()
            load_down.wait()
            for low in range(0, 4 * tile, tile):
                down_turned[low:low + tile] = down_ref[:, low:low + tile].T

        @pl.when((index >= 3) & (index < experts + 3))
        def _():
            at = index - 3
            await_bytes(rows.at[at, pl.ds(2, 2)], fc_r.at[at])
            block = join(rows[at], grids * slots)
            parts = [
                gelu(dot(block, up_ref[:, low:low + tile])).astype(BF16)
                for low in range(0, 4 * tile, tile)
            ]
            term = part(dot(jnp.concatenate(parts, axis=1), down_turned[...]), (grids,))
            own[at] = term[:2]
            part_send[at] = term[2:].astype(BF16)
            push(part_send.at[at], part_in.at[at], part_s, part_r.at[at], core)

        @pl.when(index == 3)
        def _():
            spread_far(all_image, 0)

        @pl.when((index >= 4) & (index < experts + 4))
        def _():
            at = index - 4
            await_bytes(part_in.at[at], part_r.at[at])
            sum_send[at] = (own[at, 1] + part_in[at, 1].astype(F32)).astype(BF16)
            push(sum_send.at[at], sum_in.at[at], sum_s, sum_r.at[at], cross)

        @pl.when(index >= 6)
        def _():
            at = index - 6
            await_bytes(sum_in.at[at], sum_r.at[at])
            result = own[at, 0] + part_in[at, 0].astype(F32) + sum_in[at].astype(F32)

            @pl.when(at == 0)
            def _():
                back_in[0] = result.astype(BF16)

            @pl.when(at > 0)
            def _():
                back_send[at] = result.astype(BF16)
                push(back_send.at[at], back_in.at[at], back_s, back_r, expert_peer(at))

        return carry

    lax.fori_loop(0, experts + 6, turn, 0)

    await_bytes(back_in.at[pl.ds(1, experts - 1)], back_r)
    returned = join(back_in[...], experts * slots)
    picked = dot(gate_high[...], returned) + dot(gate_low[...], returned)
    final = layer_norm(tokens_ref[...].astype(F32) + picked) * gain_ref[...]
    starts = jnp.zeros((2 * group, 1), jnp.int32)
    ends = jnp.zeros((2 * group, 1), jnp.int32)
    reached = 0
    for index in range(captions):
        starts = jnp.where(caption == index, reached, starts)
        reached = reached + lengths_ref[0, index]
        ends = jnp.where(caption == index, reached, ends)
    spot = lax.broadcasted_iota(jnp.int32, (2 * group, tokens), 1)
    members = ((spot >= starts) & (spot < ends)).astype(F32).astype(BF16)
    high, low = halves(final)
    pooled = (dot(members, high) + dot(members, low)) / jnp.maximum(ends - starts, 1).astype(F32)
    embed = root_norm(pooled)
    out_ref[0] = embed[group:group + captions]
    direction = embed / math.sqrt(width)
    near_text[0] = direction[:group].astype(BF16)
    own_text[...] = direction[group:].astype(BF16)
    share_near(near_text, 1)
    share_far(near_text, all_text, 1)

    others = pl.ds(1, experts - 1)
    spread_far(all_text, 1)
    await_far(all_image, 0)
    images_all = all_image[...].reshape(experts * group, width)
    offset = g * captions
    out_ref[1] = slope(own_text[...], images_all, offset)[:captions]
    await_far(all_text, 1)
    texts_all = all_text[...].reshape(experts * group, width)
    out_ref[2] = slope(own_image[...], texts_all, offset)[:captions]

    await_bytes(send.at[others], to_expert_s)
    await_bytes(send, fx_s)
    await_bytes(part_send, fc_s)
    await_bytes(part_send, part_s)
    await_bytes(sum_send, sum_s)
    await_bytes(back_send.at[others], back_s)
    for index, (near, every) in enumerate(((near_image, all_image), (near_text, all_text))):
        await_bytes(near.at[pl.ds(1, grids - 1)], near_s.at[index])
        await_bytes(every.at[others], far_s.at[index])


def on_device(
    tokens, routes, route_gates, caption_lengths, image_embed, final_gain, up_weight, down_weight
):
    count, width = tokens.shape
    experts, grids = lax.axis_size("expert"), lax.axis_size("grid")
    slots = 4 * count // experts
    captions = caption_lengths.shape[1]
    group = grids * captions
    inner = up_weight.shape[2]
    dma = pltpu.SemaphoreType.DMA
    whole = pl.BlockSpec(memory_space=pltpu.VMEM)
    far = pl.BlockSpec(memory_space=pl.ANY)
    out = jax.ShapeDtypeStruct((3, captions, width), F32)
    scratch = [
        pltpu.VMEM((width, inner), BF16),
        pltpu.VMEM((width, inner), BF16),
        pltpu.VMEM((inner, width), BF16),
        pltpu.VMEM((experts, slots, width), BF16),
        pltpu.VMEM((count, experts * slots), BF16),
        pltpu.VMEM((count, experts * slots), BF16),
        pltpu.VMEM((experts, grids, slots, width), BF16),
        pltpu.VMEM((experts, 2, slots, width), F32),
        pltpu.VMEM((experts, 2, slots, width), BF16),
        pltpu.VMEM((experts, 2, slots, width), BF16),
    ] + [pltpu.VMEM((experts, slots, width), BF16)] * 4 + [
        pltpu.VMEM((group, width), BF16),
        pltpu.VMEM((grids, group, width), BF16),
        pltpu.VMEM((experts, group, width), BF16),
    ] * 2 + [
        dma((2,)),
        dma, dma((experts,)),
        dma, dma((experts,)),
        dma, dma((experts,)),
        dma, dma((experts,)),
        dma, dma((experts,)),
        dma, dma,
        dma((2,)), dma((2,)), dma((2,)), dma((2,)), dma((2,)), dma((2,)),
    ]
    rows = experts * slots * grids
    result = pl.pallas_call(
        functools.partial(kernel, experts, grids, slots, captions),
        out_shape=out,
        in_specs=[pl.BlockSpec(memory_space=pltpu.SMEM)] + [whole] * 5 + [far] * 2,
        out_specs=whole,
        scratch_shapes=scratch,
        cost_estimate=pl.CostEstimate(
            flops=4 * rows * width * inner, bytes_accessed=4 * width * inner,
            transcendentals=rows * inner,
        ),
        compiler_params=pltpu.CompilerParams(
            collective_id=0, has_side_effects=True, vmem_limit_bytes=56 * 1024 * 1024
        ),
    )(
        caption_lengths, tokens, routes.T, route_gates.T, image_embed, final_gain[None, :],
        up_weight[0], down_weight[0],
    )
    return result[0], result[1], result[2]


def solution(mesh):
    split = P(("expert", "grid"), None)
    return jax.shard_map(
        on_device,
        mesh=mesh,
        in_specs=(split,) * 5 + (P(), P("expert", None, "grid"), P("expert", None, "grid")),
        out_specs=(split,) * 3,
        check_vma=False,
    )
```

profile of v0, /device:TPU:0, one launch (start us, length us, event | category | flops | bytes accessed | tf_op | source)
XLA Modules:
  0.0 81.9 jit_solution(12102768073370205547)
XLA Ops:
  0.6 79.9 %shard_map.103 = f32[3,4,1024]{2,1,0:T(4,128)} custom-call(s32[1,4]{1,0:T(1,128)} %lengths_ref.1, bf16[128,1024]{1,0:T(8,128)(2,1)} %tokens_ref.1, s32[2,128]{1,0:T(2,128)} %bitcast.14, f32[2,128]{1,0:T(2,128)} %bitcast.15, bf16[4,1024]{1,0:T(4,128)(2,1)} %image_ref.1, f32[1,1024]{1,0:T(1,128)} %bitcast.13, bf16[1024,1024]{1,0:T(8,128)(2,1)} %bitcast.11, ...), custom_call_target="tpu_custom_call" | custom-call | flops 8589934592 | bytes 4194304 | tf_op jit(solution)/shard_map/pallas_call | solution.py:369
  80.6 1.4 %slice_bitcast_fusion = (f32[4,1024]{1,0:T(4,128)}, f32[4,1024]{1,0:T(4,128)}, f32[4,1024]{1,0:T(4,128)}) fusion(f32[3,4,1024]{2,1,0:T(4,128)} %shard_map.103), kind=kLoop, calls=%fused_computation | loop fusion | bytes 98304 | tf_op jit(solution)/shard_map/squeeze | solution.py:386
where the time goes:
time: 82.2 us; the launch traced here: 81.9 us
  Pallas kernels  79.9 us (97%)
  local copies, waits for them, and re-layouts  1.37 us (2%)
    pallas_call x1, Pallas kernels, on_device(): pl.pallas_call(functools.partial(kernel, experts, grids, slots, captions)...  79.9 us

commit v1 on v0

--- a/solution.py
+++ b/solution.py
@@ -80,9 +80,9 @@
     experts, grids, slots, captions,
     lengths_ref, tokens_ref, routes_ref, gates_ref, image_ref, gain_ref, up_hbm, down_hbm,
     out_ref,
-    up_ref, down_ref, down_turned, send, gate_high, gate_low, rows, own, part_send, part_in, sum_send, sum_in,
+    up_ref, down_ref, send, gate_high, gate_low, rows, own, sum_send, sum_in,
     back_send, back_in, own_image, near_image, all_image, own_text, near_text, all_text,
-    weight_sem, to_expert_s, to_expert_r, fx_s, fx_r, fc_s, fc_r, part_s, part_r, sum_s, sum_r,
+    weight_sem, to_expert_s, to_expert_r, fx_s, fx_r, core_s, core_r, sum_s, sum_r,
     back_s, back_r, near_s, near_r, far_s, far_r, across_r, spread_r,
 ):
     e = lax.axis_index("expert")
@@ -126,9 +126,9 @@
     lax.fori_loop(1, experts, greet, 0)
     for hop in range(1, grids):
         pl.semaphore_signal(barrier, inc=1, device_id=(e, (g + hop) % grids), device_id_type=MESH)
-    load_up = pltpu.make_async_copy(up_hbm, up_ref, weight_sem.at[0])
+    load_up = pltpu.make_async_copy(up_hbm, up_ref.at[0], weight_sem.at[0])
     load_up.start()
-    load_down = pltpu.make_async_copy(down_hbm, down_ref, weight_sem.at[1])
+    load_down = pltpu.make_async_copy(down_hbm, down_ref.at[0], weight_sem.at[1])
     load_down.start()
 
     normed = layer_norm(tokens_ref[...].astype(F32)).astype(BF16)
@@ -159,7 +159,8 @@
     ahead = min(4, experts)
     lax.fori_loop(1, ahead, dispatch, 0)
     push(rows.at[0, 0], rows.at[0, 1], fx_s, fx_r.at[0], cross)
-    push(rows.at[0, 0], rows.at[0, 2], fc_s, fc_r.at[0], core)
+    push(up_hbm, up_ref.at[1], core_s.at[0], core_r.at[0], core)
+    push(down_hbm, down_ref.at[1], core_s.at[1], core_r.at[1], core)
     weights = jnp.where(hits[0], gates_ref[0:1, :], 0.0) + jnp.where(hits[1], gates_ref[1:2, :], 0.0)
     high, low = halves(weights.T)
     gate_high[...] = high
@@ -211,7 +212,7 @@
 
     share_near(near_image, 0)
 
-    tile = up_ref.shape[1] // 4
+    tile = up_ref.shape[2] // 4
 
     def turn(index, carry):
         @pl.when(index + ahead < experts)
@@ -223,52 +224,51 @@
             at = index
             await_bytes(rows.at[at, 0], to_expert_r.at[at])
             push(rows.at[at, 0], rows.at[at, 1], fx_s, fx_r.at[at], cross)
-            push(rows.at[at, 0], rows.at[at, 2], fc_s, fc_r.at[at], core)
-
-        @pl.when((index >= 2) & (index < experts + 2))
-        def _():
-            at = index - 2
-            await_bytes(rows.at[at, 1], fx_r.at[at])
-            push(rows.at[at, 1], rows.at[at, 3], fc_s, fc_r.at[at], core)
 
         @pl.when(index == 1)
         def _():
             share_far(near_image, all_image, 0)
             load_up.wait()
             load_down.wait()
-            for low in range(0, 4 * tile, tile):
-                down_turned[low:low + tile] = down_ref[:, low:low + tile].T
-
-        @pl.when((index >= 3) & (index < experts + 3))
+
+        @pl.when(index == 2)
+        def _():
+            await_bytes(up_ref.at[1], core_r.at[0])
+            await_bytes(down_ref.at[1], core_r.at[1])
+
+        @pl.when((index >= 3) & (index < experts + 3) & (index % 2 == 1))
         def _():
             at = index - 3
-            await_bytes(rows.at[at, pl.ds(2, 2)], fc_r.at[at])
-            block = join(rows[at], grids * slots)
-            parts = [
-                gelu(dot(block, up_ref[:, low:low + tile])).astype(BF16)
-                for low in range(0, 4 * tile, tile)
-            ]
-            term = part(dot(jnp.concatenate(parts, axis=1), down_turned[...]), (grids,))
-            own[at] = term[:2]
-            part_send[at] = term[2:].astype(BF16)
-            push(part_send.at[at], part_in.at[at], part_s, part_r.at[at], core)
+            both = pl.ds(at, 2)
+            for later in range(2):
+                await_bytes(rows.at[at + later, 1], fx_r.at[at + later])
+            block = join(rows[both], 4 * slots)
+            term = None
+            for side in range(2):
+                parts = [
+                    gelu(dot(block, up_ref[side, :, low:low + tile])).astype(BF16)
+                    for low in range(0, 4 * tile, tile)
+                ]
+                product = dot_nt(jnp.concatenate(parts, axis=1), down_ref[side])
+                term = product if term is None else term + product
+            term = part(term, (2, 2))
+            own[both] = term[:, 0]
+            sum_send[both] = term[:, 1].astype(BF16)
+            for later in range(2):
+                push(
+                    sum_send.at[at + later], sum_in.at[at + later], sum_s, sum_r.at[at + later],
+                    cross,
+                )
 
         @pl.when(index == 3)
         def _():
             spread_far(all_image, 0)
 
-        @pl.when((index >= 4) & (index < experts + 4))
-        def _():
-            at = index - 4
-            await_bytes(part_in.at[at], part_r.at[at])
-            sum_send[at] = (own[at, 1] + part_in[at, 1].astype(F32)).astype(BF16)
-            push(sum_send.at[at], sum_in.at[at], sum_s, sum_r.at[at], cross)
-
-        @pl.when(index >= 6)
-        def _():
-            at = index - 6
+        @pl.when(index >= 5)
+        def _():
+            at = index - 5
             await_bytes(sum_in.at[at], sum_r.at[at])
-            result = own[at, 0] + part_in[at, 0].astype(F32) + sum_in[at].astype(F32)
+            result = own[at] + sum_in[at].astype(F32)
 
             @pl.when(at == 0)
             def _():
@@ -281,7 +281,7 @@
 
         return carry
 
-    lax.fori_loop(0, experts + 6, turn, 0)
+    lax.fori_loop(0, experts + 5, turn, 0)
 
     await_bytes(back_in.at[pl.ds(1, experts - 1)], back_r)
     returned = join(back_in[...], experts * slots)
@@ -318,8 +318,8 @@
 
     await_bytes(send.at[others], to_expert_s)
     await_bytes(send, fx_s)
-    await_bytes(part_send, fc_s)
-    await_bytes(part_send, part_s)
+    await_bytes(up_ref.at[1], core_s.at[0])
+    await_bytes(down_ref.at[1], core_s.at[1])
     await_bytes(sum_send, sum_s)
     await_bytes(back_send.at[others], back_s)
     for index, (near, every) in enumerate(((near_image, all_image), (near_text, all_text))):
@@ -341,16 +341,13 @@
     far = pl.BlockSpec(memory_space=pl.ANY)
     out = jax.ShapeDtypeStruct((3, captions, width), F32)
     scratch = [
-        pltpu.VMEM((width, inner), BF16),
-        pltpu.VMEM((width, inner), BF16),
-        pltpu.VMEM((inner, width), BF16),
+        pltpu.VMEM((2, width, inner), BF16),
+        pltpu.VMEM((2, width, inner), BF16),
         pltpu.VMEM((experts, slots, width), BF16),
         pltpu.VMEM((count, experts * slots), BF16),
         pltpu.VMEM((count, experts * slots), BF16),
-        pltpu.VMEM((experts, grids, slots, width), BF16),
-        pltpu.VMEM((experts, 2, slots, width), F32),
         pltpu.VMEM((experts, 2, slots, width), BF16),
-        pltpu.VMEM((experts, 2, slots, width), BF16),
+        pltpu.VMEM((experts, slots, width), F32),
     ] + [pltpu.VMEM((experts, slots, width), BF16)] * 4 + [
         pltpu.VMEM((group, width), BF16),
         pltpu.VMEM((grids, group, width), BF16),
@@ -359,8 +356,7 @@
         dma((2,)),
         dma, dma((experts,)),
         dma, dma((experts,)),
-        dma, dma((experts,)),
-        dma, dma((experts,)),
+        dma((2,)), dma((2,)),
         dma, dma((experts,)),
         dma, dma,
         dma((2,)), dma((2,)), dma((2,)), dma((2,)), dma((2,)), dma((2,)),

time: 82.2 us -> 83.2 us (1.012)
  Pallas kernels: 79.9 us -> 81 us
    pallas_call x1, Pallas kernels: 79.9 us -> 81 us  [on_device(): pl.pallas_call(functools.partial(kernel, experts, grids, slots, captions)...]
where the time goes in v1:
time: 83.2 us; the launch traced here: 83 us
  Pallas kernels  81 us (97%)
  local copies, waits for them, and re-layouts  1.37 us (2%)
    pallas_call x1, Pallas kernels, on_device(): pl.pallas_call(functools.partial(kernel, experts, grids, slots, captions)...  81 us

profile of v1, /device:TPU:0, one launch (start us, length us, event | category | flops | bytes accessed | tf_op | source)
XLA Modules:
  0.0 83.0 jit_solution(8261765424115878163)
XLA Ops:
  0.6 81.0 %shard_map.103 = f32[3,4,1024]{2,1,0:T(4,128)} custom-call(s32[1,4]{1,0:T(1,128)} %lengths_ref.1, bf16[128,1024]{1,0:T(8,128)(2,1)} %tokens_ref.1, s32[2,128]{1,0:T(2,128)} %bitcast.14, f32[2,128]{1,0:T(2,128)} %bitcast.15, bf16[4,1024]{1,0:T(4,128)(2,1)} %image_ref.1, f32[1,1024]{1,0:T(1,128)} %bitcast.13, bf16[1024,1024]{1,0:T(8,128)(2,1)} %bitcast.11, ...), custom_call_target="tpu_custom_call" | custom-call | flops 8589934592 | bytes 4194304 | tf_op jit(solution)/shard_map/pallas_call | solution.py:365
  81.6 1.4 %slice_bitcast_fusion = (f32[4,1024]{1,0:T(4,128)}, f32[4,1024]{1,0:T(4,128)}, f32[4,1024]{1,0:T(4,128)}) fusion(f32[3,4,1024]{2,1,0:T(4,128)} %shard_map.103), kind=kLoop, calls=%fused_computation | loop fusion | bytes 98304 | tf_op jit(solution)/shard_map/squeeze | solution.py:382

commit v2 on v1

--- a/solution.py
+++ b/solution.py
@@ -126,6 +126,9 @@
     lax.fori_loop(1, experts, greet, 0)
     for hop in range(1, grids):
         pl.semaphore_signal(barrier, inc=1, device_id=(e, (g + hop) % grids), device_id_type=MESH)
+    pl.semaphore_wait(barrier, experts + grids - 2)
+    push(up_hbm, up_ref.at[1], core_s.at[0], core_r.at[0], core)
+    push(down_hbm, down_ref.at[1], core_s.at[1], core_r.at[1], core)
     load_up = pltpu.make_async_copy(up_hbm, up_ref.at[0], weight_sem.at[0])
     load_up.start()
     load_down = pltpu.make_async_copy(down_hbm, down_ref.at[0], weight_sem.at[1])
@@ -150,7 +153,6 @@
     blocks = part(dot(taken, normed), (experts,)).astype(BF16)
     send[...] = blocks
     rows[0, 0] = blocks[0]
-    pl.semaphore_wait(barrier, experts + grids - 2)
 
     def dispatch(step, carry):
         push(send.at[step], rows.at[step, 0], to_expert_s, to_expert_r.at[step], expert_peer(step))
@@ -159,8 +161,6 @@
     ahead = min(4, experts)
     lax.fori_loop(1, ahead, dispatch, 0)
     push(rows.at[0, 0], rows.at[0, 1], fx_s, fx_r.at[0], cross)
-    push(up_hbm, up_ref.at[1], core_s.at[0], core_r.at[0], core)
-    push(down_hbm, down_ref.at[1], core_s.at[1], core_r.at[1], core)
     weights = jnp.where(hits[0], gates_ref[0:1, :], 0.0) + jnp.where(hits[1], gates_ref[1:2, :], 0.0)
     high, low = halves(weights.T)
     gate_high[...] = high
@@ -228,11 +228,11 @@
         @pl.when(index == 1)
         def _():
             share_far(near_image, all_image, 0)
+
+        @pl.when(index == 3)
+        def _():
             load_up.wait()
             load_down.wait()
-
-        @pl.when(index == 2)
-        def _():
             await_bytes(up_ref.at[1], core_r.at[0])
             await_bytes(down_ref.at[1], core_r.at[1])
 

time: 83.2 us -> 83.9 us (level)
  no operation moved by 1% of the time
where the time goes in v2:
time: 83.9 us; the launch traced here: 83.7 us
  Pallas kernels  81.7 us (97%)
  local copies, waits for them, and re-layouts  1.37 us (2%)
    pallas_call x1, Pallas kernels, on_device(): pl.pallas_call(functools.partial(kernel, experts, grids, slots, captions)...  81.7 us

profile of v2, /device:TPU:0, one launch (start us, length us, event | category | flops | bytes accessed | tf_op | source)
XLA Modules:
  0.0 83.7 jit_solution(7640447453151911895)
XLA Ops:
  0.6 81.7 %shard_map.103 = f32[3,4,1024]{2,1,0:T(4,128)} custom-call(s32[1,4]{1,0:T(1,128)} %lengths_ref.1, bf16[128,1024]{1,0:T(8,128)(2,1)} %tokens_ref.1, s32[2,128]{1,0:T(2,128)} %bitcast.14, f32[2,128]{1,0:T(2,128)} %bitcast.15, bf16[4,1024]{1,0:T(4,128)(2,1)} %image_ref.1, f32[1,1024]{1,0:T(1,128)} %bitcast.13, bf16[1024,1024]{1,0:T(8,128)(2,1)} %bitcast.11, ...), custom_call_target="tpu_custom_call" | custom-call | flops 8589934592 | bytes 4194304 | tf_op jit(solution)/shard_map/pallas_call | solution.py:365
  82.4 1.4 %slice_bitcast_fusion = (f32[4,1024]{1,0:T(4,128)}, f32[4,1024]{1,0:T(4,128)}, f32[4,1024]{1,0:T(4,128)}) fusion(f32[3,4,1024]{2,1,0:T(4,128)} %shard_map.103), kind=kLoop, calls=%fused_computation | loop fusion | bytes 98304 | tf_op jit(solution)/shard_map/squeeze | solution.py:382
